TPU v7x, 32 devices: a whole 2x2x4 slice. The times are simulated.
32 devices in a mesh: dp: 8 (over z, core), mp: 4 (over y, x).
Axes of the slice: x: 2, y: 2, z: 4, core: 2. Of those that a mesh axis runs over, the one named last changes fastest.
Arguments:
- visual: bfloat16 [256, 8, 6144], P('dp', None, 'mp'), may hold values from -6 to 6
- vis_gain: float32 [6144], replicated, may hold values from 0.1 to 1.9
- text: bfloat16 [256, 8, 4096], P(None, 'dp'), may hold values from -6 to 6
- text_gain: float32 [4096], replicated, may hold values from 0.1 to 1.9
- query_weight: bfloat16 [4096, 4096], P(None, 'mp'), may hold values from -0.375 to 0.375
- key_weight: bfloat16 [6144, 4096], P(None, 'mp'), may hold values from -0.078125 to 0.078125
- value_weight: bfloat16 [6144, 4096], P(None, 'mp'), may hold values from -0.078125 to 0.078125
- out_weight: bfloat16 [4096, 4096], P('mp'), may hold values from -0.09375 to 0.09375
Outputs:
- mixed: bfloat16 [256, 8, 4096], P('mp', 'dp')
All inputs are finite; a program needn't handle non-finite values.
Results may differ from a plain program's by a relative error of at most 0.015.
Values may be sent and summed in bfloat16 or wider, within the bound.
A program may use at most 128 MiB of HBM per device.

v0:
```python
import jax
import jax.numpy as jnp
from jax import lax
from jax.sharding import PartitionSpec as P

DEC = 4096
HEAD_DIM = 128


epsilon = 1e-06


def layer_norm(values, gain):
    average = jnp.mean(values, axis=-1, keepdims=True)
    centred = values - average
    spread = jnp.mean(centred * centred, axis=-1, keepdims=True)
    return centred * lax.rsqrt(spread + epsilon) * gain


def body(visual, vis_gain, text, text_gain, query_weight, key_weight, value_weight, out_weight):
    relayed = lax.all_to_all(visual, "dp", split_axis=1, concat_axis=0, tiled=True)
    vis_tokens, images_here, feature_count = relayed.shape
    full_width = feature_count * lax.axis_size("mp")
    vis_rows = vis_tokens * images_here
    kv_columns = key_weight.shape[1]
    whole = lax.all_gather(relayed, "mp", axis=2, tiled=True)
    normed = layer_norm(whole.astype(jnp.float32), vis_gain).astype(jnp.bfloat16)
    normed = normed.reshape(vis_rows, full_width)
    keys = jnp.dot(normed, key_weight, preferred_element_type=jnp.float32).astype(jnp.bfloat16)
    values = jnp.dot(normed, value_weight, preferred_element_type=jnp.float32).astype(jnp.bfloat16)
    heads_here = kv_columns // HEAD_DIM
    text_tokens = text.shape[0]
    text_f = text.astype(jnp.float32)
    text_norm = (
        text_f * lax.rsqrt(jnp.mean(text_f * text_f, axis=-1, keepdims=True) + epsilon) * text_gain
    ).astype(jnp.bfloat16)
    queries = jnp.dot(
        text_norm.reshape(text_tokens * images_here, DEC),
        query_weight,
        preferred_element_type=jnp.float32,
    ).astype(jnp.bfloat16)
    queries = queries.reshape(text_tokens, images_here, heads_here, HEAD_DIM)
    keys = keys.reshape(vis_tokens, images_here, heads_here, HEAD_DIM)
    values = values.reshape(vis_tokens, images_here, heads_here, HEAD_DIM)
    scores = jnp.einsum(
        "tihd,vihd->ihtv", queries, keys, preferred_element_type=jnp.float32
    ) / jnp.sqrt(jnp.float32(HEAD_DIM))
    probs = jax.nn.softmax(scores, axis=-1).astype(jnp.bfloat16)
    context = jnp.einsum(
        "ihtv,vihd->tihd", probs, values, preferred_element_type=jnp.float32
    ).astype(jnp.bfloat16)
    context = context.reshape(text_tokens * images_here, kv_columns)
    summed = lax.psum_scatter(
        jnp.dot(context, out_weight, preferred_element_type=jnp.float32).astype(jnp.bfloat16),
        "mp",
        scatter_dimension=0,
        tiled=True,
    ).astype(jnp.float32)
    tokens_here = text_tokens // lax.axis_size("mp")
    residual = lax.dynamic_slice_in_dim(text, lax.axis_index("mp") * tokens_here, tokens_here, 0)
    return (residual.astype(jnp.float32) + summed.reshape(tokens_here, images_here, DEC)).astype(
        jnp.bfloat16
    )


def solution(mesh):
    in_specs = (
        P("dp", None, "mp"),
        P(),
        P(None, "dp", None),
        P(),
        P(None, "mp"),
        P(None, "mp"),
        P(None, "mp"),
        P("mp", None),
    )
    out_specs = P("mp", "dp", None)
    return jax.shard_map(body, mesh=mesh, in_specs=in_specs, out_specs=out_specs, check_vma=False)
```

profile of v0, /device:TPU:0, one launch (start us, length us, event | category | flops | bytes accessed | tf_op | source)
XLA Modules:
  0.0 156.7 jit_solution(11887084034790303365)
XLA Ops:
  6.5 0.0 copy-start.1
  6.5 0.0 copy-start.3
  6.5 0.0 all-gather.2.cloned.1.call-start
  6.5 1.5 copy.13
  8.1 27.2 %all_to_all.18 = bf16[32,8,1536]{2,0,1:T(8,128)(2,1)} all-to-all(bf16[32,8,1536]{2,0,1:T(8,128)(2,1)S(1)} %copy.13), channel_id=1, replica_groups=mesh['dp'=8,'mp'=4] {'dp'}, dimensions={1} | all-to-all | bytes 1572864 | tf_op jit(solution)/shard_map/all_to_all | solution.py:21
  35.3 0.0 all-gather.2.cloned.1.call-update
  35.3 0.0 reduce-scatter.2.cloned.1.call-start
  35.3 0.0 copy-done.1
  35.3 0.5 fusion.6
  35.9 0.0 copy-done.3
  35.9 6.6 %fusion.20 = bf16[32,8,8,128]{3,2,1,0:T(8,128)(2,1)} fusion(bf16[4096,1024]{1,0:T(8,128)(2,1)} %param.12, bf16[256,1,4096]{2,0,1:T(8,128)(2,1)S(1)} %copy-done.1, f32[4096]{0:T(1024)S(1)} %copy-done.3, f32[256]{0:T(256)S(1)} %add_rsqrt_fusion), kind=kOutput, calls=%fused_computation.28 | convolution fusion | flops 2151940096 | bytes 11027456 | tf_op jit(solution)/shard_map/dot_general | solution.py:37
  42.4 35.9 %all-gather.2.cloned.1.call-done = bf16[256,1,6144]{2,0,1:T(8,128)(2,1)} async-done(((bf16[256,1,1536]{2,0,1:T(8,128)(2,1)}), bf16[256,1,6144]{2,0,1:T(8,128)(2,1)}) %all-gather.2.cloned.1.call-update) | async-done | bytes 3145744 | tf_op jit(solution)/shard_map/all_gather | solution.py:26
  78.3 0.0 copy-start
  78.3 0.0 copy-start.2
  78.3 2.5 %convert_reduce_fusion = f32[256]{0:T(256)S(1)} fusion(bf16[256,1,6144]{2,0,1:T(8,128)(2,1)} %all-gather.2.cloned.1.call-done), kind=kLoop, calls=%fused_computation.2 | loop fusion | flops 3145472 | bytes 3146752 | tf_op jit(solution)/shard_map/reduce_sum | solution.py:14
  80.9 0.3 copy-done
  81.2 1.0 fusion.3
  82.1 0.0 copy-done.2
  82.2 8.8 %convolution_convert_fusion.2 = bf16[256,1024]{1,0:T(8,128)(2,1)} fusion(bf16[6144,1024]{1,0:T(8,128)(2,1)} %param.14, bf16[256,1,6144]{2,0,1:T(8,128)(2,1)S(1)} %copy-done, f32[6144]{0:T(1024)S(1)} %copy-done.2, f32[256]{0:T(256)S(1)} %add_rsqrt_fusion.1, f32[256]{0:T(256)S(1)} %broadcast_multiply_fusion), kind=kOutput, calls=%fused_computation.25 | convolution fusion | flops 3229351936 | bytes 16279552 | tf_op jit(solution)/shard_map/dot_general | solution.py:30
  91.0 2.0 %copy.19 = bf16[256,1024]{0,1:T(8,128)(2,1)} copy(bf16[256,1024]{1,0:T(8,128)(2,1)} %convolution_convert_fusion.2) | data formatting | bytes 1048576 | tf_op jit(solution)/shard_map/reshape.19
  93.0 8.8 %fusion.19 = bf16[32,8,8,128]{3,2,1,0:T(8,128)(2,1)} fusion(bf16[6144,1024]{1,0:T(8,128)(2,1)} %param.13, bf16[256,1,6144]{2,0,1:T(8,128)(2,1)S(1)} %copy-done, f32[6144]{0:T(1024)S(1)} %copy-done.2, f32[256]{0:T(256)S(1)} %add_rsqrt_fusion.1, f32[256]{0:T(256)S(1)} %broadcast_multiply_fusion), kind=kOutput, calls=%fused_computation.27 | convolution fusion | flops 3229351936 | bytes 16279552 | tf_op jit(solution)/shard_map/dot_general | solution.py:29
  101.9 2.0 %fusion.45 = (f32[8,256]{1,0:T(8,128)S(1)}, f32[8,256,256]{1,2,0:T(8,128)S(1)}) fusion(bf16[32,8,8,128]{3,2,1,0:T(8,128)(2,1)} %fusion.19, bf16[32,8,8,128]{3,2,1,0:T(8,128)(2,1)} %fusion.20), kind=kOutput, calls=%fused_computation.41 | convolution fusion | flops 135790848 | bytes 3153920 | tf_op jit(solution)/shard_map/sub | solution.py:48
  103.9 1.4 convolution_convert_fusion.3
  105.3 7.1 %convolution_convert_fusion = bf16[256,4096]{1,0:T(8,128)(2,1)} fusion(bf16[256,1024]{0,1:T(8,128)(2,1)S(1)} %bitcast.58, bf16[1024,4096]{1,0:T(8,128)(2,1)} %param.15), kind=kOutput, calls=%fused_computation.10 | convolution fusion | flops 2148532224 | bytes 11010048 | tf_op jit(solution)/shard_map/dot_general | solution.py:54
  112.4 0.0 reduce-scatter.2.cloned.1.call-update
  112.4 35.4 %reduce-scatter.2.cloned.1.call-done = bf16[64,4096]{1,0:T(8,128)(2,1)} async-done(((bf16[256,4096]{1,0:T(8,128)(2,1)}), bf16[64,4096]{1,0:T(8,128)(2,1)}) %reduce-scatter.2.cloned.1.call-update) | async-done | bytes 524304 | tf_op jit(solution)/shard_map/reduce_scatter | solution.py:53
  147.8 2.1 %fusion.23 = bf16[64,1,4096]{2,0,1:T(8,128)(2,1)} fusion(bf16[64,4096]{1,0:T(8,128)(2,1)} %reduce-scatter.2.cloned.1.call-done, bf16[256,1,4096]{2,0,1:T(8,128)(2,1)} %param.10, s32[]{:T(128)S(6)} %select_n.3), kind=kLoop, calls=%fused_computation.30 | loop fusion | flops 1048576 | bytes 1572868 | tf_op jit(solution)/shard_map/convert_element_type | solution.py:61
  (3 shorter events, 0.0 us)
Async XLA Ops:
  6.5 28.8 %copy-start.1 = (bf16[256,1,4096]{2,0,1:T(8,128)(2,1)S(1)}, bf16[256,1,4096]{2,0,1:T(8,128)(2,1)}, u32[]{:S(2)}) copy-start(bf16[256,1,4096]{2,0,1:T(8,128)(2,1)} %param.10) | copy-start | bytes 6291460
  6.5 29.3 %copy-start.3 = (f32[4096]{0:T(1024)S(1)}, f32[4096]{0:T(1024)}, u32[]{:S(2)}) copy-start(f32[4096]{0:T(1024)} %param.11) | copy-start | bytes 49156
  6.5 71.8 %all-gather.2.cloned.1.call-start = ((), (), s32[]{:S(2)}) async-start(), calls=%async_computation.2 | async-start | bytes 3932160 | tf_op jit(solution)/shard_map/all_gather | solution.py:26
  35.3 112.5 %reduce-scatter.2.cloned.1.call-start = ((), (), s32[]{:S(2)}) async-start(), calls=%async_computation.3 | async-start | bytes 2621440 | tf_op jit(solution)/shard_map/reduce_scatter | solution.py:53
  78.3 2.8 %copy-start = (bf16[256,1,6144]{2,0,1:T(8,128)(2,1)S(1)}, bf16[256,1,6144]{2,0,1:T(8,128)(2,1)}, u32[]{:S(2)}) copy-start(bf16[256,1,6144]{2,0,1:T(8,128)(2,1)} %all-gather.2.cloned.1.call-done) | copy-start | bytes 9437188
  78.3 3.8 %copy-start.2 = (f32[6144]{0:T(1024)S(1)}, f32[6144]{0:T(1024)}, u32[]{:S(2)}) copy-start(f32[6144]{0:T(1024)} %param.9) | copy-start | bytes 73732
Sparse Core Ops, SparseCore 0:
  35.4 42.8 all-gather.1
  112.5 35.2 reduce-scatter.1
where the time goes:
time: 157 us
  waiting for transfers between devices  71.3 us (45%)
  matrix products  34.7 us (22%)
  blocking collectives  27.2 us (17%)
  between operations  13.4 us (9%)
  other arithmetic  6.14 us (4%)
  local copies, waits for them, and re-layouts  3.84 us (2%)
    all_gather x1, waiting for transfers between devices, body(): whole = lax.all_gather(relayed, 'mp', axis=2, tiled=True)  35.9 us
    reduce_scatter x1, waiting for transfers between devices, body(): lax.psum_scatter(jnp.dot(context, out_weight, preferred_element_type=jnp....  35.4 us
    all_to_all x1, blocking collectives, body(): lax.all_to_all(visual, 'dp', split_axis=1, concat_axis=0, tiled=True)  27.2 us
    dot_general x1, matrix products, body(): jnp.dot(normed, key_weight, preferred_element_type=jnp.float32)  8.84 us
    dot_general x1, matrix products, body(): jnp.dot(normed, value_weight, preferred_element_type=jnp.float32)  8.84 us
    dot_general x1, matrix products, body(): jnp.dot(context, out_weight, preferred_element_type=jnp.float32)  7.11 us
    dot_general x1, matrix products, body(): jnp.dot(text_norm.reshape(text_tokens * images_here, DEC), query_weight,...  6.57 us
  transfers between devices with their start and end apart: 2, of which 2 were waited for; matrix products, arithmetic and copies ran while one was open for 5% of the time, Pallas kernels for 0%

commit v1 on v0

--- a/solution.py
+++ b/solution.py
@@ -1,6 +1,10 @@
+import functools
+
 import jax
 import jax.numpy as jnp
 from jax import lax
+from jax.experimental import pallas as pl
+from jax.experimental.pallas import tpu as pltpu
 from jax.sharding import PartitionSpec as P
 
 DEC = 4096
@@ -17,7 +21,7 @@
     return centred * lax.rsqrt(spread + epsilon) * gain
 
 
-def body(visual, vis_gain, text, text_gain, query_weight, key_weight, value_weight, out_weight):
+def plain_body(visual, vis_gain, text, text_gain, query_weight, key_weight, value_weight, out_weight):
     relayed = lax.all_to_all(visual, "dp", split_axis=1, concat_axis=0, tiled=True)
     vis_tokens, images_here, feature_count = relayed.shape
     full_width = feature_count * lax.axis_size("mp")
@@ -63,6 +67,329 @@
     )
 
 
+def flipped(index, mask):
+    result, bit = index, 1
+    while bit <= mask:
+        if mask & bit:
+            result = result + bit - 2 * bit * lax.rem(lax.div(index, bit), 2)
+        bit *= 2
+    return result
+
+
+def fused_kernel(
+    n, vis_ref, vis_gain_ref, text_gain_ref, text_hbm, wq_hbm, wk_hbm, wv_hbm, wo_hbm, out_ref,
+    gathered, normed, text_ref, text_norm, wq, wk, wv, wo, queries, keys, values, context,
+    partial, first_in, second_out, second_in,
+    local_sem, z_send, z_recv, x_send, x_recv, y_send, y_recv, d_send, d_recv,
+    s1_send, s1_recv, s2_send, s2_recv,
+):
+    d, m = lax.axis_index("dp"), lax.axis_index("mp")
+    x, y = lax.rem(m, 2), lax.div(m, 2)
+    xm, ym = m + 1 - 2 * x, m + 2 - 4 * y
+    block, features = vis_ref.shape[1], vis_ref.shape[2]
+    columns = queries.shape[1]
+    chunks, _, _, out_rows, chunk = partial.shape
+
+    loads = [
+        pltpu.make_async_copy(source, target, local_sem.at[i])
+        for i, (source, target) in enumerate(
+            [(text_hbm, text_ref), (wq_hbm, wq), (wk_hbm, wk), (wv_hbm, wv), (wo_hbm, wo)]
+        )
+    ]
+    for load in loads:
+        load.start()
+
+    barrier = pltpu.get_barrier_semaphore()
+    peers = [(flipped(d, k), m) for k in range(1, n)] + [(d, xm), (d, ym)]
+    for peer in peers:
+        pl.semaphore_signal(barrier, inc=1, device_id=peer, device_id_type=pl.DeviceIdType.MESH)
+    pl.semaphore_wait(barrier, len(peers))
+
+    def send(source, target, send_sem, recv_sem, device):
+        return pltpu.make_async_remote_copy(
+            src_ref=source, dst_ref=target, send_sem=send_sem, recv_sem=recv_sem,
+            device_id=device, device_id_type=pl.DeviceIdType.MESH,
+        )
+
+    def rows(k):
+        return pl.ds(k * block, block)
+
+    def z_copy(k):
+        target = flipped(d, k)
+        return send(
+            vis_ref.at[target], gathered.at[m, rows(k)], z_send.at[k], z_recv.at[k], (target, m)
+        )
+
+    def x_copy(k):
+        mine = gathered.at[m, rows(k)]
+        return send(mine, mine, x_send.at[k], x_recv.at[k], (d, xm))
+
+    def y_copy(k):
+        mine = gathered.at[m, rows(k)]
+        return send(mine, mine, y_send.at[k], y_recv.at[k], (d, ym))
+
+    def relay(k):
+        if k % 2 == 0:
+            part = gathered.at[xm, rows(k)]
+            return send(part, part, d_send.at[k], d_recv.at[k], (d, ym))
+        part = gathered.at[ym, rows(k)]
+        return send(part, part, d_send.at[k], d_recv.at[k], (d, xm))
+
+    def spread(k):
+        if k > 0:
+            z_copy(k).wait_recv()
+        x_copy(k).start()
+        y_copy(k).start()
+
+    def pass_on(k):
+        (x_copy if k % 2 == 0 else y_copy)(k).wait_recv()
+        relay(k).start()
+
+    def normalize(k):
+        (y_copy if k % 2 == 0 else x_copy)(k).wait_recv()
+        relay(k).wait_recv()
+        parts = gathered.shape[0]
+
+        def piece(i, carry):
+            here = pl.ds(pl.multiple_of(k * block + i * 16, 16), 16)
+            total = jnp.zeros((16, 1), jnp.float32)
+            for q in range(parts):
+                total += jnp.sum(gathered[q, here].astype(jnp.float32), axis=-1, keepdims=True)
+            average = total / (parts * features)
+            spread_of = jnp.zeros((16, 1), jnp.float32)
+            for q in range(parts):
+                centred = gathered[q, here].astype(jnp.float32) - average
+                spread_of += jnp.sum(centred * centred, axis=-1, keepdims=True)
+            scale = lax.rsqrt(spread_of / (parts * features) + epsilon)
+            for q in range(parts):
+                span = slice(q * features, (q + 1) * features)
+                centred = gathered[q, here].astype(jnp.float32) - average
+                normed[here, span] = (centred * scale * vis_gain_ref[:, span]).astype(jnp.bfloat16)
+            return carry
+
+        lax.fori_loop(0, block // 16, piece, 0)
+
+    gathered[m, rows(0)] = vis_ref[d]
+    spread(0)
+    for k in range(1, n):
+        z_copy(k).start()
+
+    tile = min(256, columns)
+    tiles = columns // tile
+
+    def tile_at(j):
+        return pl.ds(pl.multiple_of(j * tile, tile), tile)
+
+    def text_piece(i, carry):
+        here = pl.ds(pl.multiple_of(i * 16, 16), 16)
+        piece = text_ref[here].astype(jnp.float32)
+        mean = jnp.mean(piece * piece, axis=-1, keepdims=True)
+        text_norm[here] = (piece * lax.rsqrt(mean + epsilon) * text_gain_ref[...]).astype(
+            jnp.bfloat16
+        )
+        return carry
+
+    def query_tile(j, carry):
+        queries[:, tile_at(j)] = jnp.dot(
+            text_norm[...], wq[:, tile_at(j)], preferred_element_type=jnp.float32
+        ).astype(jnp.bfloat16)
+        return carry
+
+    def kv_tiles(span):
+        def one(j, carry):
+            keys[span, tile_at(j)] = jnp.dot(
+                normed[span], wk[:, tile_at(j)], preferred_element_type=jnp.float32
+            ).astype(jnp.bfloat16)
+            values[span, tile_at(j)] = jnp.dot(
+                normed[span], wv[:, tile_at(j)], preferred_element_type=jnp.float32
+            ).astype(jnp.bfloat16)
+            return carry
+
+        return one
+
+    spread(1)
+    loads[0].wait()
+    lax.fori_loop(0, text_ref.shape[0] // 16, text_piece, 0)
+    pass_on(0)
+    for k in range(2, n):
+        spread(k)
+        pass_on(k - 1)
+        if k == 2:
+            loads[1].wait()
+        lower, upper = (k - 2) * tiles // (n - 2), (k - 1) * tiles // (n - 2)
+        if n == 2:
+            lower, upper = 0, tiles
+        if upper > lower:
+            lax.fori_loop(lower, upper, query_tile, 0)
+        if k >= n // 2 + 1:
+            normalize(k - n // 2 - 1)
+    if n == 2:
+        loads[1].wait()
+        lax.fori_loop(0, tiles, query_tile, 0)
+    half = n // 2
+    for k in range(half):
+        if k < n // 2 + 1 and not (n > 2 and k <= n - 1 - n // 2 - 1):
+            normalize(k)
+    loads[2].wait()
+    loads[3].wait()
+    first, second = pl.ds(0, half * block), pl.ds(half * block, half * block)
+    lax.fori_loop(0, tiles // 2, kv_tiles(first), 0)
+    pass_on(n - 1)
+    lax.fori_loop(tiles // 2, tiles, kv_tiles(first), 0)
+    for k in range(half, n):
+        normalize(k)
+    lax.fori_loop(0, tiles, kv_tiles(second), 0)
+
+    for h in range(columns // HEAD_DIM):
+        span = slice(h * HEAD_DIM, (h + 1) * HEAD_DIM)
+        scores = lax.dot_general(
+            queries[:, span], keys[:, span], (((1,), (1,)), ((), ())),
+            preferred_element_type=jnp.float32,
+        ) * (HEAD_DIM ** -0.5)
+        weights = jnp.exp(scores - jnp.max(scores, axis=-1, keepdims=True))
+        total = jnp.sum(weights, axis=-1, keepdims=True)
+        mixed = jnp.dot(
+            weights.astype(jnp.bfloat16), values[:, span], preferred_element_type=jnp.float32
+        )
+        context[:, span] = (mixed / total).astype(jnp.bfloat16)
+
+    loads[4].wait()
+
+    def order(c):
+        if c % 2 == 0:
+            return x, y, (d, xm), (d, ym)
+        return y, x, (d, ym), (d, xm)
+
+    def first_copy(c):
+        a, _, near, _ = order(c)
+        return send(partial.at[c, 1 - a], first_in.at[c], s1_send.at[c], s1_recv.at[c], near)
+
+    def second_copy(c):
+        return send(second_out.at[c], second_in.at[c], s2_send.at[c], s2_recv.at[c], order(c)[3])
+
+    def project(c):
+        product = jnp.dot(
+            context[...], wo[:, c * chunk : (c + 1) * chunk], preferred_element_type=jnp.float32
+        ).astype(jnp.bfloat16)
+        for r in range(4):
+            a, b = (r % 2, r // 2) if c % 2 == 0 else (r // 2, r % 2)
+            partial[c, a, b] = product[r * out_rows : (r + 1) * out_rows]
+        first_copy(c).start()
+
+    def turn(c):
+        a, b, _, _ = order(c)
+        first_copy(c).wait_recv()
+        second_out[c] = (
+            partial[c, a, 1 - b].astype(jnp.float32) + first_in[c, 1 - b].astype(jnp.float32)
+        ).astype(jnp.bfloat16)
+        second_copy(c).start()
+
+    def finish(c):
+        a, b, _, _ = order(c)
+        second_copy(c).wait_recv()
+        span = slice(c * chunk, (c + 1) * chunk)
+        residual = text_ref[pl.ds(pl.multiple_of(m * out_rows, 16), out_rows), span]
+        out_ref[:, span] = (
+            residual.astype(jnp.float32)
+            + partial[c, a, b].astype(jnp.float32)
+            + first_in[c, b].astype(jnp.float32)
+            + second_in[c].astype(jnp.float32)
+        ).astype(jnp.bfloat16)
+
+    for c in range(chunks):
+        project(c)
+        if c >= 3:
+            turn(c - 3)
+    for c in range(max(chunks - 3, 0), chunks):
+        turn(c)
+    for c in range(chunks):
+        finish(c)
+
+    for k in range(n):
+        if k > 0:
+            z_copy(k).wait_send()
+        x_copy(k).wait_send()
+        y_copy(k).wait_send()
+        relay(k).wait_send()
+    for c in range(chunks):
+        first_copy(c).wait_send()
+        second_copy(c).wait_send()
+
+
+def fused_body(n, visual, vis_gain, text, text_gain, query_weight, key_weight, value_weight, out_weight):
+    block, _, features = visual.shape
+    tokens, _, width = text.shape
+    columns = key_weight.shape[1]
+    vis_rows, vis_width = block * n, features * 4
+    out_rows = tokens // 4
+    chunks = 8
+    chunk = width // chunks
+    bf16 = jnp.bfloat16
+    sems = [pltpu.SemaphoreType.DMA((5,))]
+    sems += [pltpu.SemaphoreType.DMA((n,))] * 8 + [pltpu.SemaphoreType.DMA((chunks,))] * 4
+    vmem = pl.BlockSpec(memory_space=pltpu.VMEM)
+    anywhere = pl.BlockSpec(memory_space=pl.ANY)
+    result = pl.pallas_call(
+        functools.partial(fused_kernel, n),
+        out_shape=jax.ShapeDtypeStruct((out_rows, width), bf16),
+        in_specs=[vmem] * 3 + [anywhere] * 5,
+        out_specs=vmem,
+        scratch_shapes=[
+            pltpu.VMEM((4, vis_rows, features), bf16),
+            pltpu.VMEM((vis_rows, vis_width), bf16),
+            pltpu.VMEM((tokens, width), bf16),
+            pltpu.VMEM((tokens, width), bf16),
+            pltpu.VMEM(query_weight.shape, bf16),
+            pltpu.VMEM(key_weight.shape, bf16),
+            pltpu.VMEM(value_weight.shape, bf16),
+            pltpu.VMEM(out_weight.shape, bf16),
+            pltpu.VMEM((tokens, columns), bf16),
+            pltpu.VMEM((vis_rows, columns), bf16),
+            pltpu.VMEM((vis_rows, columns), bf16),
+            pltpu.VMEM((tokens, columns), bf16),
+            pltpu.VMEM((chunks, 2, 2, out_rows, chunk), bf16),
+            pltpu.VMEM((chunks, 2, out_rows, chunk), bf16),
+            pltpu.VMEM((chunks, out_rows, chunk), bf16),
+            pltpu.VMEM((chunks, out_rows, chunk), bf16),
+        ]
+        + sems,
+        compiler_params=pltpu.CompilerParams(
+            collective_id=0, has_side_effects=True, vmem_limit_bytes=63 * 2**20
+        ),
+    )(
+        jnp.transpose(visual, (1, 0, 2)),
+        vis_gain.reshape(1, vis_width),
+        text_gain.reshape(1, width),
+        text.reshape(tokens, width),
+        query_weight,
+        key_weight,
+        value_weight,
+        out_weight,
+    )
+    return result.reshape(out_rows, 1, width)
+
+
+def body(visual, *rest):
+    n, groups = lax.axis_size("dp"), lax.axis_size("mp")
+    text, columns = rest[1], rest[4].shape[1]
+    block, images, features = visual.shape
+    fits = (
+        groups == 4
+        and n >= 2
+        and n & (n - 1) == 0
+        and images == n
+        and block % 16 == 0
+        and features % 128 == 0
+        and columns % HEAD_DIM == 0
+        and (columns < 256 or columns % 256 == 0)
+        and text.shape[0] % 64 == 0
+        and text.shape[2] % 1024 == 0
+    )
+    if fits:
+        return fused_body(n, visual, *rest)
+    return plain_body(visual, *rest)
+
+
 def solution(mesh):
     in_specs = (
         P("dp", None, "mp"),

time: 157 us -> 72.7 us (0.46)
  waiting for transfers between devices: 71.3 us -> 0 us
  Pallas kernels: 0 us -> 68.4 us
  matrix products: 34.7 us -> 0 us
  blocking collectives: 27.2 us -> 0 us
  between operations: 13.4 us -> 0.01 us
  other arithmetic: 6.14 us -> 0 us
    pallas_call x0 -> x1, Pallas kernels: none -> 68.4 us  [fused_body(): pl.pallas_call(functools.partial(fused_kernel, n), out_shape=jax.ShapeDty...]
    all_gather x1 -> x0, waiting for transfers between devices: 35.9 us -> none  [body(): whole = lax.all_gather(relayed, 'mp', axis=2, tiled=True)]
    reduce_scatter x1 -> x0, waiting for transfers between devices: 35.4 us -> none  [body(): lax.psum_scatter(jnp.dot(context, out_weight, preferred_element_type=jnp....]
    dot_general x5 -> x0, matrix products: 32.7 us -> none  [the longest x1 8.84 us: body(): jnp.dot(normed, key_weight, preferred_element_type=jnp.float32)]
    all_to_all x1 -> x0, blocking collectives: 27.2 us -> none  [body(): lax.all_to_all(visual, 'dp', split_axis=1, concat_axis=0, tiled=True)]
    reduce_sum x3 -> x0, other arithmetic: 4 us -> none  [the longest x1 2.54 us: layer_norm(): average = jnp.mean(values, axis=-1, keepdims=True)]
    unnamed x9 -> x2, local copies, waits for them, and re-layouts: 1.81 us -> 4.11 us
    convert_element_type x1 -> x0, other arithmetic: 2.11 us -> none  [body(): (residual.astype(jnp.float32) + summed.reshape(tokens_here, images_here,...]
  transfers between devices with their start and end apart: 2 -> 0, of which waited for: 2 -> 0; matrix products, arithmetic and copies ran while one was open for 5% -> 0% of each run, Pallas kernels for 0% -> 0%
where the time goes in v1:
time: 72.7 us; the launch traced here: 72.5 us
  Pallas kernels  68.4 us (94%)
  local copies, waits for them, and re-layouts  4.11 us (6%)
    pallas_call x1, Pallas kernels, fused_body(): pl.pallas_call(functools.partial(fused_kernel, n), out_shape=jax.ShapeDty...  68.4 us
    unnamed x2, local copies, waits for them, and re-layouts  4.11 us

profile of v1, /device:TPU:0, one launch (start us, length us, event | category | flops | bytes accessed | tf_op | source)
XLA Modules:
  0.0 72.5 jit_solution(5687441941746299387)
XLA Ops:
  0.0 2.2 %copy.11 = bf16[32,8,1536]{2,0,1:T(8,128)(2,1)} copy(bf16[32,8,1536]{2,1,0:T(8,128)(2,1)} %param.8) | data formatting | bytes 1572864 | tf_op args[0]
  2.2 68.4 %shard_map.82 = bf16[64,4096]{1,0:T(8,128)(2,1)} custom-call(bf16[8,32,1536]{2,1,0:T(8,128)(2,1)} %bitcast.7, f32[1,6144]{1,0:T(1,128)} %bitcast.10, f32[1,4096]{1,0:T(1,128)} %bitcast.11, bf16[256,4096]{1,0:T(8,128)(2,1)} %bitcast.9, bf16[4096,1024]{1,0:T(8,128)(2,1)} %wq_hbm.1, bf16[6144,1024]{1,0:T(8,128)(2,1)} %wk_hbm.1, bf16[6144,1024]{1,0:T(8,128)(2,1)} %wv_hbm.1, ...), custom_call_target="tpu_custom_call" | custom-call | tf_op jit(solution)/shard_map/pallas_call | solution.py:332
  70.7 1.9 %copy.13 = bf16[64,1,4096]{2,0,1:T(8,128)(2,1)} copy(bf16[64,1,4096]{2,0,1:T(8,128)(2,1)} %bitcast.8) | data formatting | bytes 1048576

commit v2 on v1

--- a/solution.py
+++ b/solution.py
@@ -128,12 +128,19 @@
         mine = gathered.at[m, rows(k)]
         return send(mine, mine, y_send.at[k], y_recv.at[k], (d, ym))
 
-    def relay(k):
-        if k % 2 == 0:
-            part = gathered.at[xm, rows(k)]
-            return send(part, part, d_send.at[k], d_recv.at[k], (d, ym))
-        part = gathered.at[ym, rows(k)]
-        return send(part, part, d_send.at[k], d_recv.at[k], (d, xm))
+    def relays(k):
+        half = features // 2
+        both = k == n - 1
+        copies = []
+        if both or k % 2 == 0:
+            part = gathered.at[xm, rows(k), pl.ds(0, half if both else features)]
+            copies.append(send(part, part, d_send.at[k], d_recv.at[k], (d, ym)))
+        if both or k % 2 == 1:
+            start = half if both else 0
+            part = gathered.at[ym, rows(k), pl.ds(start, features - start)]
+            slot = n if both else k
+            copies.append(send(part, part, d_send.at[slot], d_recv.at[slot], (d, xm)))
+        return copies
 
     def spread(k):
         if k > 0:
@@ -142,12 +149,18 @@
         y_copy(k).start()
 
     def pass_on(k):
-        (x_copy if k % 2 == 0 else y_copy)(k).wait_recv()
-        relay(k).start()
+        if k % 2 == 0 or k == n - 1:
+            x_copy(k).wait_recv()
+        if k % 2 == 1 or k == n - 1:
+            y_copy(k).wait_recv()
+        for copy in relays(k):
+            copy.start()
 
     def normalize(k):
-        (y_copy if k % 2 == 0 else x_copy)(k).wait_recv()
-        relay(k).wait_recv()
+        if k < n - 1:
+            (y_copy if k % 2 == 0 else x_copy)(k).wait_recv()
+        for copy in relays(k):
+            copy.wait_recv()
         parts = gathered.shape[0]
 
         def piece(i, carry):
@@ -310,7 +323,8 @@
             z_copy(k).wait_send()
         x_copy(k).wait_send()
         y_copy(k).wait_send()
-        relay(k).wait_send()
+        for copy in relays(k):
+            copy.wait_send()
     for c in range(chunks):
         first_copy(c).wait_send()
         second_copy(c).wait_send()
@@ -326,7 +340,8 @@
     chunk = width // chunks
     bf16 = jnp.bfloat16
     sems = [pltpu.SemaphoreType.DMA((5,))]
-    sems += [pltpu.SemaphoreType.DMA((n,))] * 8 + [pltpu.SemaphoreType.DMA((chunks,))] * 4
+    sems += [pltpu.SemaphoreType.DMA((n,))] * 6 + [pltpu.SemaphoreType.DMA((n + 1,))] * 2
+    sems += [pltpu.SemaphoreType.DMA((chunks,))] * 4
     vmem = pl.BlockSpec(memory_space=pltpu.VMEM)
     anywhere = pl.BlockSpec(memory_space=pl.ANY)
     result = pl.pallas_call(
@@ -379,7 +394,7 @@
         and n & (n - 1) == 0
         and images == n
         and block % 16 == 0
-        and features % 128 == 0
+        and features % 256 == 0
         and columns % HEAD_DIM == 0
         and (columns < 256 or columns % 256 == 0)
         and text.shape[0] % 64 == 0

time: 72.7 us -> 72.8 us (level)
  no operation moved by 1% of the time
where the time goes in v2:
time: 72.8 us; the launch traced here: 72.5 us
  Pallas kernels  68.4 us (94%)
  local copies, waits for them, and re-layouts  4.11 us (6%)
    pallas_call x1, Pallas kernels, fused_body(): pl.pallas_call(functools.partial(fused_kernel, n), out_shape=jax.ShapeDty...  68.4 us
    unnamed x2, local copies, waits for them, and re-layouts  4.11 us

profile of v2, /device:TPU:0, one launch (start us, length us, event | category | flops | bytes accessed | tf_op | source)
XLA Modules:
  0.0 72.5 jit_solution(10199005636328012859)
XLA Ops:
  0.0 2.2 %copy.11 = bf16[32,8,1536]{2,0,1:T(8,128)(2,1)} copy(bf16[32,8,1536]{2,1,0:T(8,128)(2,1)} %param.8) | data formatting | bytes 1572864 | tf_op args[0]
  2.2 68.4 %shard_map.82 = bf16[64,4096]{1,0:T(8,128)(2,1)} custom-call(bf16[8,32,1536]{2,1,0:T(8,128)(2,1)} %bitcast.7, f32[1,6144]{1,0:T(1,128)} %bitcast.10, f32[1,4096]{1,0:T(1,128)} %bitcast.11, bf16[256,4096]{1,0:T(8,128)(2,1)} %bitcast.9, bf16[4096,1024]{1,0:T(8,128)(2,1)} %wq_hbm.1, bf16[6144,1024]{1,0:T(8,128)(2,1)} %wk_hbm.1, bf16[6144,1024]{1,0:T(8,128)(2,1)} %wv_hbm.1, ...), custom_call_target="tpu_custom_call" | custom-call | tf_op jit(solution)/shard_map/pallas_call | solution.py:347
  70.7 1.9 %copy.13 = bf16[64,1,4096]{2,0,1:T(8,128)(2,1)} copy(bf16[64,1,4096]{2,0,1:T(8,128)(2,1)} %bitcast.8) | data formatting | bytes 1048576
